TPU v7x, 128 devices: a whole 4x4x4 slice. The times are simulated.
128 devices in a mesh: prow: 8 (over x_lo, z), pcol: 16 (over y, x_hi, core).
Axes of the slice: x: 4 (x_hi: 2, x_lo: 2; x = x_hi * 2 + x_lo), y: 4, z: 4, core: 2. Of those that a mesh axis runs over, the one named last changes fastest.
Arguments:
- values: float32 [12, 8, 4, 16, 256, 256], P(None, 'prow', None, 'pcol'), may hold values from -6 to 6
- pattern: int32 [12, 8, 4, 16], P(None, 'prow', None, 'pcol'), may hold values from 0 to 1
Outputs:
- factored: float32 [12, 8, 4, 16, 256, 256], P(None, 'prow', None, 'pcol')
All inputs are finite; a program needn't handle non-finite values.
Results may differ from a plain program's by a relative error of at most 0.0003.
Values sent between devices are 32-bit elements; how exact they have to be, the bound alone decides.
A program may use at most 128 MiB of HBM per device.

v0:
```python
import math
import jax
import jax.numpy as jnp
from jax import lax
from jax.sharding import Mesh
from jax.sharding import PartitionSpec as P

SWEEPS = 3
PROW = ("prow_0", "prow_1")
shift_coef = 5.0


def picked(value, axis, root):
    return lax.dynamic_index_in_dim(lax.all_gather(value, axis), root, 0, keepdims=False)


def rows_for(lines, peers):
    spare = -lines.shape[0] % peers
    if not spare:
        return lines
    return jnp.concatenate([lines, jnp.zeros((spare, *lines.shape[1:]), lines.dtype)])


def spread(value, axis, root):
    lines = jnp.where(lax.axis_index(axis) == root, value, jnp.zeros_like(value)).reshape(
        -1, *value.shape[1:][-1:]
    )
    padded = rows_for(lines, lax.axis_size(axis))
    own = lax.psum_scatter(padded, axis, scatter_dimension=0, tiled=True)
    return lax.all_gather(own, axis, axis=0, tiled=True)[: len(lines)].reshape(value.shape)


def broadcast_by_axis(value, axes, root):
    value = jnp.where(lax.axis_index(axes) == root, value, jnp.zeros_like(value))
    for axis in axes:
        value = lax.psum(value, axis)
    return value


def newton(block, shift):
    width = block.shape[0]
    eye = jnp.eye(width, dtype=jnp.float32)
    approx = eye / shift
    for step in range(SWEEPS):
        inner = jnp.dot(block, approx, precision=lax.Precision.HIGHEST)
        approx = jnp.dot(approx, 2.0 * eye - inner, precision=lax.Precision.HIGHEST)
    return approx


def spread_inverse(block, shift, root_row):
    return picked(newton(block, shift), PROW, root_row)


def apply_panel(blocks, rows_g, cols_g, mult, upper, k):
    product = jnp.einsum("rab,cbe->rcae", mult, upper, precision=lax.Precision.HIGHEST)
    below = rows_g > k
    trail = (below[:, None] & (cols_g > k)[None, :])[:, :, None, None]
    store = (below[:, None] & (cols_g == k)[None, :])[:, :, None, None]
    out = jnp.where(trail, blocks - product, blocks)
    return jnp.where(store, mult[:, None], out)


def drop_one(array, index, axis_pos):
    return jnp.concatenate(
        [
            lax.slice_in_dim(array, 0, index, axis=axis_pos),
            lax.slice_in_dim(array, index + 1, array.shape[axis_pos], axis=axis_pos),
        ],
        axis=axis_pos,
    )


def put_one(array, piece, index, axis_pos):
    return jnp.concatenate(
        [lax.slice_in_dim(array, 0, index, axis=axis_pos), piece, array], axis=axis_pos
    )


def factor_panel(column, row, k, shift, nprow, npcol):
    root_row, loc_row = (k % nprow, k // nprow)
    root_col = k % npcol
    column = spread(column, "pcol", root_col)
    inverse = spread_inverse(column[loc_row], shift, root_row)
    mult = jnp.einsum("rab,be->rae", column, inverse, precision=lax.Precision.HIGHEST)
    upper = broadcast_by_axis(row, PROW, root_row)
    return (mult, upper)


def body(values, pattern):
    rows_loc, cols_loc, width = (values.shape[0], values.shape[2], values.shape[4])
    nprow = lax.axis_size(PROW)
    npcol = lax.axis_size("pcol")
    rows_g = jnp.arange(rows_loc, dtype=jnp.int32) * nprow + lax.axis_index(PROW)
    cols_g = jnp.arange(cols_loc, dtype=jnp.int32) * npcol + lax.axis_index("pcol")
    shift = shift_coef * math.sqrt(width)
    eye = jnp.eye(width, dtype=jnp.float32)
    blocks = values[:, 0, :, 0] * pattern[:, 0, :, 0].astype(jnp.float32)[:, :, None, None]
    diag = jnp.where(rows_g[:, None] == cols_g[None, :], shift, 0.0).astype(jnp.float32)
    blocks = blocks + diag[:, :, None, None] * eye
    row_first, col_first = (0 // nprow, 0 // npcol)
    row_next, col_next = (1 // nprow, 1 // npcol)
    mult_first, upper_first = factor_panel(
        blocks[:, col_first], blocks[row_first], 0, shift, nprow, npcol
    )
    column = apply_panel(
        blocks[:, col_next : col_next + 1],
        rows_g,
        cols_g[col_next : col_next + 1],
        mult_first,
        upper_first[col_next : col_next + 1],
        0,
    )[:, 0]
    row = apply_panel(
        blocks[row_next : row_next + 1],
        rows_g[row_next : row_next + 1],
        cols_g,
        mult_first[row_next : row_next + 1],
        upper_first,
        0,
    )[0]
    mult_next, upper_next = factor_panel(column, row, 1, shift, nprow, npcol)
    inner = drop_one(drop_one(blocks, row_next, 0), col_next, 1)
    inner = apply_panel(
        inner,
        drop_one(rows_g, row_next, 0),
        drop_one(cols_g, col_next, 0),
        drop_one(mult_first, row_next, 0),
        drop_one(upper_first, col_next, 0),
        0,
    )
    inner = put_one(inner, drop_one(column, row_next, 0)[:, None], col_next, 1)
    blocks = put_one(inner, row[None], row_next, 0)
    blocks = apply_panel(blocks, rows_g, cols_g, mult_next, upper_next, 1)
    return blocks[:, None, :, None]


def solution(mesh):
    torus = Mesh(mesh.devices.reshape(2, 4, mesh.shape["pcol"]), ("prow_0", "prow_1", "pcol"))
    return jax.shard_map(
        body,
        mesh=torus,
        in_specs=(P(None, PROW, None, "pcol", None, None), P(None, PROW, None, "pcol")),
        out_specs=P(None, PROW, None, "pcol", None, None),
        check_vma=False,
    )
```

profile of v0, /device:TPU:0, one launch (start us, length us, event | category | flops | bytes accessed | tf_op | source)
XLA Modules:
  0.0 466.2 jit_solution(778879318605547930)
XLA Ops:
  8.2 12.2 %fusion.2 = f32[12,4,256,256]{3,2,0,1:T(8,128)} fusion(f32[12,1,4,1,256,256]{5,4,3,2,1,0:T(8,128)} %param.2, f32[256,256]{1,0:T(8,128)S(1)} %fusion.18, f32[12,4]{0,1:T(4,128)S(1)} %compare_select_fusion, f32[12,4]{0,1:T(4,128)S(1)} %bitcast.93), kind=kLoop, calls=%fused_computation.5 | loop fusion | flops 9437184 | bytes 25428352 | tf_op jit(solution)/shard_map/add | solution.py:99
  20.4 3.8 slice_select_fusion
  24.2 77.9 %reduce-scatter.3.cloned.1.call-done = f32[192,256]{1,0:T(8,128)} async-done(((f32[3072,256]{1,0:T(8,128)}), f32[192,256]{1,0:T(8,128)}) %reduce-scatter.3.cloned.1.call-update) | async-done | bytes 196624 | tf_op jit(solution)/shard_map/reduce_scatter | solution.py:29
  102.2 2.3 select_bitcast_fusion.1
  104.6 63.7 %all-gather.7.cloned.1.call-done = f32[3072,256]{1,0:T(8,128)} async-done(((f32[192,256]{1,0:T(8,128)}), f32[3072,256]{1,0:T(8,128)}) %all-gather.7.cloned.1.call-update) | async-done | bytes 3145744 | tf_op jit(solution)/shard_map/all_gather | solution.py:30
  169.9 1.3 convolution_subtract_fusion.4
  171.7 1.3 convolution_subtract_fusion.3
  174.8 43.0 %all-gather.11.cloned.1.call-done = f32[2048,256]{1,0:T(8,128)} async-done(((f32[256,256]{1,0:T(8,128)}), f32[2048,256]{1,0:T(8,128)}) %all-gather.11.cloned.1.call-update) | async-done | bytes 2097168 | tf_op jit(solution)/shard_map/all_gather | solution.py:14
  217.9 4.6 fusion.16
  222.4 9.0 %all-reduce.7.cloned.1.call-done = f32[4,256,256]{2,1,0:T(8,128)} async-done(((f32[4,256,256]{2,1,0:T(8,128)}), f32[4,256,256]{2,1,0:T(8,128)}) %all-reduce.7.cloned.1.call-update) | async-done | bytes 1048592 | tf_op jit(solution)/shard_map/psum | solution.py:36
  231.4 6.1 %broadcast_select_fusion = (f32[12,1,256,256]{3,2,0,1:T(8,128)}, f32[12,1,256,256]{3,2,0,1:T(8,128)}) fusion(pred[]{:T(512)S(6)} %eq.80, f32[12,256,256]{2,1,0:T(8,128)S(1)} %fusion.16, f32[4,256,256]{2,1,0:T(8,128)} %all-reduce.7.cloned.1.call-done, f32[12,4,256,256]{3,2,0,1:T(8,128)} %fusion.2, pred[12]{0:T(512)(128)(4,1)S(1)} %get-tuple-element.13, ...), kind=kOutput, calls=%fused_computation.13 | convolution fusion | flops 2419064832 | bytes 15991809 | tf_op jit(solution)/shard_map/rab,cbe->rcae/dot_general | solution.py:55
  237.6 75.6 %reduce-scatter.5.cloned.1.call-done = f32[192,256]{1,0:T(8,128)} async-done(((f32[3072,256]{1,0:T(8,128)}), f32[192,256]{1,0:T(8,128)}) %reduce-scatter.5.cloned.1.call-update) | async-done | bytes 196624 | tf_op jit(solution)/shard_map/reduce_scatter | solution.py:29
  313.4 2.7 fusion.7
  318.5 46.7 %all-gather.9.cloned.1.call-done = f32[3072,256]{1,0:T(8,128)} async-done(((f32[192,256]{1,0:T(8,128)}), f32[3072,256]{1,0:T(8,128)}) %all-gather.9.cloned.1.call-update) | async-done | bytes 3145744 | tf_op jit(solution)/shard_map/all_gather | solution.py:30
  365.2 1.3 convolution_subtract_fusion.2
  367.0 1.3 convolution_subtract_fusion.1
  371.6 1.5 copy-done.1
  373.1 1.9 slice.75
  376.0 12.7 %fusion.3 = f32[11,3,256,256]{3,2,0,1:T(8,128)} fusion(f32[12,4,256,256]{3,2,0,1:T(8,128)} %fusion.2, f32[11,256,256]{2,1,0:T(8,128)S(1)} %slice-done, pred[11,3]{0,1:T(4,128)(4,1)S(1)} %get-tuple-element.8, pred[11,3]{0,1:T(4,128)(4,1)S(1)} %get-tuple-element.7, f32[4,256,256]{2,1,0:T(8,128)} %all-reduce.7.cloned.1.call-done), kind=kOutput, calls=%fused_computation.6 | convolution fusion | flops 6650265600 | bytes 23856128 | tf_op jit(solution)/shard_map/rab,cbe->rcae/dot_general | solution.py:55
  388.7 26.7 %all-gather.13.cloned.1.call-done = f32[2048,256]{1,0:T(8,128)} async-done(((f32[256,256]{1,0:T(8,128)}), f32[2048,256]{1,0:T(8,128)}) %all-gather.13.cloned.1.call-update) | async-done | bytes 2097168 | tf_op jit(solution)/shard_map/all_gather | solution.py:14
  415.4 6.4 %fusion.15 = f32[12,256,256]{2,1,0:T(8,128)} fusion(f32[12,256,256]{2,1,0:T(8,128)} %bitcast.91, f32[2048,256]{1,0:T(8,128)} %all-gather.13.cloned.1.call-done), kind=kOutput, calls=%fused_computation.33 | convolution fusion | flops 2415919104 | bytes 6553600 | tf_op jit(solution)/shard_map/rab,be->rae/dot_general | solution.py:84
  421.7 7.9 %all-reduce.11.cloned.1.call-done = f32[4,256,256]{2,1,0:T(8,128)} async-done(((f32[4,256,256]{2,1,0:T(8,128)}), f32[4,256,256]{2,1,0:T(8,128)}) %all-reduce.11.cloned.1.call-update) | async-done | bytes 1048592 | tf_op jit(solution)/shard_map/psum | solution.py:36
  429.7 18.2 %fusion.1 = f32[12,1,4,1,256,256]{5,4,0,2,3,1:T(8,128)} fusion(f32[11,3,256,256]{3,2,0,1:T(8,128)} %fusion.3, f32[11,1,256,256]{3,2,0,1:T(8,128)} %slice.75, f32[1,4,256,256]{3,2,0,1:T(8,128)S(1)} %copy-done.3, f32[12,256,256]{2,1,0:T(8,128)} %fusion.15, pred[12,4]{0,1:T(4,128)(4,1)S(1)} %get-tuple-element.6, pred[12,4]{0,1:T(4,128)(4,1)S(1)} %get-tuple-element.5, ...), kind=kOutput, calls=%fused_computation.3 | convolution fusion | flops 9679405056 | bytes 29360224 | tf_op jit(solution)/shard_map/rab,cbe->rcae/dot_general | solution.py:55
  447.9 10.8 %copy.10 = f32[12,1,4,1,256,256]{5,4,3,2,1,0:T(8,128)} copy(f32[12,1,4,1,256,256]{5,4,0,2,3,1:T(8,128)} %fusion.1) | data formatting | bytes 25165824 | tf_op jit(solution)/shard_map/broadcast_in_dim | solution.py:134
  (54 shorter events, 11.8 us)
Async XLA Ops:
  7.4 94.8 %reduce-scatter.3.cloned.1.call-start = ((), (), s32[]{:S(2)}) async-start(), calls=%async_computation.2 | async-start | bytes 3342336 | tf_op jit(solution)/shard_map/reduce_scatter | solution.py:29
  24.2 144.0 %all-gather.7.cloned.1.call-start = ((), (), s32[]{:S(2)}) async-start(), calls=%async_computation.3 | async-start | bytes 3342336 | tf_op jit(solution)/shard_map/all_gather | solution.py:30
  102.2 72.0 %all-reduce.5.cloned.1.call-start = ((), (), s32[]{:S(2)}) async-start(), calls=%async_computation.4 | async-start | bytes 2097152 | tf_op jit(solution)/shard_map/psum | solution.py:36
  104.5 113.3 %all-gather.11.cloned.1.call-start = ((), (), s32[]{:S(2)}) async-start(), calls=%async_computation.10 | async-start | bytes 2359296 | tf_op jit(solution)/shard_map/all_gather | solution.py:14
  174.1 57.3 %all-reduce.7.cloned.1.call-start = ((), (), s32[]{:S(2)}) async-start(), calls=%async_computation.5 | async-start | bytes 2097152 | tf_op jit(solution)/shard_map/psum | solution.py:36
  174.7 138.5 %reduce-scatter.5.cloned.1.call-start = ((), (), s32[]{:S(2)}) async-start(), calls=%async_computation.6 | async-start | bytes 3342336 | tf_op jit(solution)/shard_map/reduce_scatter | solution.py:29
  222.4 149.1 %copy-start = (f32[12,256,256]{2,1,0:T(8,128)}, f32[12,256,256]{2,1,0:T(8,128)S(1)}, u32[]{:S(2)}) copy-start(f32[12,256,256]{2,1,0:T(8,128)S(1)} %fusion.16) | copy-start | bytes 9437188
  237.5 127.7 %all-gather.9.cloned.1.call-start = ((), (), s32[]{:S(2)}) async-start(), calls=%async_computation.7 | async-start | bytes 3342336 | tf_op jit(solution)/shard_map/all_gather | solution.py:30
  313.2 61.8 %all-reduce.9.cloned.1.call-start = ((), (), s32[]{:S(2)}) async-start(), calls=%async_computation.8 | async-start | bytes 2097152 | tf_op jit(solution)/shard_map/psum | solution.py:36
  316.0 1.1 copy-start.2
  318.3 97.1 %all-gather.13.cloned.1.call-start = ((), (), s32[]{:S(2)}) async-start(), calls=%async_computation.11 | async-start | bytes 2359296 | tf_op jit(solution)/shard_map/all_gather | solution.py:14
  371.2 58.5 %all-reduce.11.cloned.1.call-start = ((), (), s32[]{:S(2)}) async-start(), calls=%async_computation.9 | async-start | bytes 2097152 | tf_op jit(solution)/shard_map/psum | solution.py:36
  371.2 1.9 copy-start.1
  373.1 2.9 slice-start
  415.4 14.3 %copy-start.3 = (f32[1,4,256,256]{3,2,0,1:T(8,128)S(1)}, f32[1,4,256,256]{3,2,0,1:T(8,128)}, u32[]{:S(2)}) copy-start(f32[1,4,256,256]{3,2,0,1:T(8,128)} %copy-done.2) | copy-start | bytes 3145732
Sparse Core Ops, SparseCore 0:
  24.3 77.7 reduce-scatter.2
  104.6 63.5 all-gather.6
  174.2 43.5 all-gather.10
  237.7 75.4 reduce-scatter.4
  315.5 49.6 all-gather.8
  371.3 44.0 all-gather.12
Sparse Core Ops, SparseCore 1:
  105.1 45.9 all-reduce.4
  177.1 54.3 all-reduce.6
  318.4 49.1 all-reduce.8
  375.1 54.5 all-reduce.10
where the time goes:
time: 467 us; the launch traced here: 466 us
  waiting for transfers between devices  351 us (75%)
  matrix products  62.3 us (13%)
  other arithmetic  20.5 us (4%)
  local copies, waits for them, and re-layouts  16.2 us (3%)
  between operations  15.4 us (3%)
    reduce_scatter x2, waiting for transfers between devices, spread(): own = lax.psum_scatter(padded, axis, scatter_dimension=0, tiled=True)  153 us
    all_gather x2, waiting for transfers between devices, spread(): lax.all_gather(own, axis, axis=0, tiled=True)[:len(lines)]  110 us
    all_gather x2, waiting for transfers between devices, picked(): lax.all_gather(value, axis)  69.7 us
    dot_general x4, matrix products, apply_panel(): jnp.einsum('rab,cbe->rcae', mult, upper, precision=lax.Precision.HIGHEST)  39.7 us
    psum x4, waiting for transfers between devices, broadcast_by_axis(): value = lax.psum(value, axis)  16.9 us
    add x1, other arithmetic, body(): blocks = blocks + diag[:, :, None, None] * eye  12.2 us
    dot_general x2, matrix products, factor_panel(): jnp.einsum('rab,be->rae', column, inverse, precision=lax.Precision.HIGHEST)  10.9 us
    broadcast_in_dim x1, local copies, waits for them, and re-layouts, body(): return blocks[:, None, :, None]  10.8 us
  transfers between devices with their start and end apart: 10, of which 8 were waited for; matrix products, arithmetic and copies ran while one was open for 9% of the time, Pallas kernels for 0%

commit v1 on v0

--- a/solution.py
+++ b/solution.py
@@ -33,7 +33,7 @@
 def broadcast_by_axis(value, axes, root):
     value = jnp.where(lax.axis_index(axes) == root, value, jnp.zeros_like(value))
     for axis in axes:
-        value = lax.psum(value, axis)
+        value = jnp.sum(lax.all_gather(value, axis), axis=0)
     return value
 
 

time: 467 us -> 517 us (1.11)
  waiting for transfers between devices: 351 us -> 396 us
  other arithmetic: 20.5 us -> 32.3 us
    all_gather x0 -> x4, waiting for transfers between devices: none -> 69.7 us  [broadcast_by_axis(): value = jnp.sum(lax.all_gather(value, axis), axis=0)]
    all_gather x2, waiting for transfers between devices: 110 us -> 93 us  [spread(): lax.all_gather(own, axis, axis=0, tiled=True)[:len(lines)]]
    psum x4 -> x0, waiting for transfers between devices: 16.9 us -> none  [broadcast_by_axis(): value = lax.psum(value, axis)]
    reduce_sum x0 -> x4, other arithmetic: none -> 12.9 us  [broadcast_by_axis(): value = jnp.sum(lax.all_gather(value, axis), axis=0)]
    all_gather x2, waiting for transfers between devices: 69.7 us -> 80.2 us  [picked(): lax.all_gather(value, axis)]
where the time goes in v1:
time: 517 us
  waiting for transfers between devices  396 us (77%)
  matrix products  58.6 us (11%)
  other arithmetic  32.3 us (6%)
  between operations  15.3 us (3%)
  local copies, waits for them, and re-layouts  14.3 us (3%)
    reduce_scatter x2, waiting for transfers between devices, spread(): own = lax.psum_scatter(padded, axis, scatter_dimension=0, tiled=True)  153 us
    all_gather x2, waiting for transfers between devices, spread(): lax.all_gather(own, axis, axis=0, tiled=True)[:len(lines)]  93 us
    all_gather x2, waiting for transfers between devices, picked(): lax.all_gather(value, axis)  80.2 us
    all_gather x4, waiting for transfers between devices, broadcast_by_axis(): value = jnp.sum(lax.all_gather(value, axis), axis=0)  69.7 us
    dot_general x4, matrix products, apply_panel(): jnp.einsum('rab,cbe->rcae', mult, upper, precision=lax.Precision.HIGHEST)  38.7 us
    reduce_sum x4, other arithmetic, broadcast_by_axis(): value = jnp.sum(lax.all_gather(value, axis), axis=0)  12.9 us
    add x1, other arithmetic, body(): blocks = blocks + diag[:, :, None, None] * eye  12.2 us
    broadcast_in_dim x1, local copies, waits for them, and re-layouts, body(): return blocks[:, None, :, None]  10.8 us
  transfers between devices with their start and end apart: 10, of which 8 were waited for; matrix products, arithmetic and copies ran while one was open for 9% of the time, Pallas kernels for 0%

profile of v1, /device:TPU:0, one launch (start us, length us, event | category | flops | bytes accessed | tf_op | source)
XLA Modules:
  0.0 516.6 jit_solution(17868791792121970804)
XLA Ops:
  8.2 12.2 %fusion.2 = f32[12,4,256,256]{3,2,0,1:T(8,128)} fusion(f32[12,1,4,1,256,256]{5,4,3,2,1,0:T(8,128)} %param.2, f32[256,256]{1,0:T(8,128)S(1)} %fusion.18, f32[12,4]{0,1:T(4,128)S(1)} %compare_select_fusion, f32[12,4]{0,1:T(4,128)S(1)} %bitcast.95), kind=kLoop, calls=%fused_computation.5 | loop fusion | flops 9437184 | bytes 25428352 | tf_op jit(solution)/shard_map/add | solution.py:99
  20.4 3.8 slice_select_fusion
  24.3 2.3 slice_select_fusion.1
  26.6 77.9 %reduce-scatter.3.cloned.1.call-done = f32[192,256]{1,0:T(8,128)} async-done(((f32[3072,256]{1,0:T(8,128)}), f32[192,256]{1,0:T(8,128)}) %reduce-scatter.3.cloned.1.call-update) | async-done | bytes 196624 | tf_op jit(solution)/shard_map/reduce_scatter | solution.py:29
  104.6 2.8 reduce_sum.36
  107.5 46.6 %all-gather.13.cloned.1.call-done = f32[3072,256]{1,0:T(8,128)} async-done(((f32[192,256]{1,0:T(8,128)}), f32[3072,256]{1,0:T(8,128)}) %all-gather.13.cloned.1.call-update) | async-done | bytes 3145744 | tf_op jit(solution)/shard_map/all_gather | solution.py:30
  160.1 42.7 %all-gather.23.cloned.1.call-done = f32[16,256,256]{2,1,0:T(8,128)} async-done(((f32[4,256,256]{2,1,0:T(8,128)}), f32[16,256,256]{2,1,0:T(8,128)}) %all-gather.23.cloned.1.call-update) | async-done | bytes 4194320 | tf_op jit(solution)/shard_map/all_gather | solution.py:36
  202.8 3.6 reduce_sum.37
  206.4 40.2 %all-gather.21.cloned.1.call-done = f32[2048,256]{1,0:T(8,128)} async-done(((f32[256,256]{1,0:T(8,128)}), f32[2048,256]{1,0:T(8,128)}) %all-gather.21.cloned.1.call-update) | async-done | bytes 2097168 | tf_op jit(solution)/shard_map/all_gather | solution.py:14
  246.6 4.5 fusion.16
  251.1 7.3 %broadcast_select_fusion = (f32[12,1,256,256]{3,2,0,1:T(8,128)}, f32[12,1,256,256]{3,2,0,1:T(8,128)}) fusion(pred[]{:T(512)S(6)} %eq.80, f32[12,256,256]{2,1,0:T(8,128)S(1)} %fusion.16, f32[4,256,256]{2,1,0:T(8,128)} %reduce_sum.37, f32[12,4,256,256]{3,2,0,1:T(8,128)} %fusion.2, pred[12]{0:T(512)(128)(4,1)S(1)} %get-tuple-element.15, ...), kind=kOutput, calls=%fused_computation.13 | convolution fusion | flops 2419064832 | bytes 15991809 | tf_op jit(solution)/shard_map/rab,cbe->rcae/dot_general | solution.py:55
  258.6 4.1 broadcast_select_fusion.1
  262.7 74.7 %reduce-scatter.5.cloned.1.call-done = f32[192,256]{1,0:T(8,128)} async-done(((f32[3072,256]{1,0:T(8,128)}), f32[192,256]{1,0:T(8,128)}) %reduce-scatter.5.cloned.1.call-update) | async-done | bytes 196624 | tf_op jit(solution)/shard_map/reduce_scatter | solution.py:29
  337.8 2.9 reduce_sum.38
  340.7 46.4 %all-gather.17.cloned.1.call-done = f32[3072,256]{1,0:T(8,128)} async-done(((f32[192,256]{1,0:T(8,128)}), f32[3072,256]{1,0:T(8,128)}) %all-gather.17.cloned.1.call-update) | async-done | bytes 3145744 | tf_op jit(solution)/shard_map/all_gather | solution.py:30
  393.3 1.5 copy-done.1
  394.9 1.9 slice.75
  396.8 12.1 %fusion.3 = f32[11,3,256,256]{3,2,0,1:T(8,128)} fusion(f32[12,4,256,256]{3,2,0,1:T(8,128)} %fusion.2, f32[11,256,256]{2,1,0:T(8,128)S(1)} %slice-done, pred[11,3]{0,1:T(4,128)(4,1)S(1)} %get-tuple-element.8, pred[11,3]{0,1:T(4,128)(4,1)S(1)} %get-tuple-element.7, f32[4,256,256]{2,1,0:T(8,128)S(1)} %copy-done.2), kind=kOutput, calls=%fused_computation.6 | convolution fusion | flops 6650265600 | bytes 23856128 | tf_op jit(solution)/shard_map/rab,cbe->rcae/dot_general | solution.py:55
  408.9 26.9 %all-gather.27.cloned.1.call-done = f32[16,256,256]{2,1,0:T(8,128)} async-done(((f32[4,256,256]{2,1,0:T(8,128)}), f32[16,256,256]{2,1,0:T(8,128)}) %all-gather.27.cloned.1.call-update) | async-done | bytes 4194320 | tf_op jit(solution)/shard_map/all_gather | solution.py:36
  435.8 3.6 reduce_sum.39
  439.4 40.1 %all-gather.25.cloned.1.call-done = f32[2048,256]{1,0:T(8,128)} async-done(((f32[256,256]{1,0:T(8,128)}), f32[2048,256]{1,0:T(8,128)}) %all-gather.25.cloned.1.call-update) | async-done | bytes 2097168 | tf_op jit(solution)/shard_map/all_gather | solution.py:14
  479.4 3.7 fusion.15
  483.2 15.2 %fusion.1 = f32[12,1,4,1,256,256]{5,4,0,2,3,1:T(8,128)} fusion(f32[11,3,256,256]{3,2,0,1:T(8,128)} %fusion.3, f32[11,1,256,256]{3,2,0,1:T(8,128)S(1)} %copy-done.4, f32[1,4,256,256]{3,2,0,1:T(8,128)S(1)} %copy-done.5, f32[12,256,256]{2,1,0:T(8,128)S(1)} %fusion.15, pred[12,4]{0,1:T(4,128)(4,1)S(1)} %get-tuple-element.6, ...), kind=kOutput, calls=%fused_computation.3 | convolution fusion | flops 9679405056 | bytes 29360224 | tf_op jit(solution)/shard_map/rab,cbe->rcae/dot_general | solution.py:55
  498.4 10.8 %copy.24 = f32[12,1,4,1,256,256]{5,4,3,2,1,0:T(8,128)} copy(f32[12,1,4,1,256,256]{5,4,0,2,3,1:T(8,128)} %fusion.1) | data formatting | bytes 25165824 | tf_op jit(solution)/shard_map/broadcast_in_dim | solution.py:134
  (63 shorter events, 13.6 us)
Async XLA Ops:
  7.4 97.1 %reduce-scatter.3.cloned.1.call-start = ((), (), s32[]{:S(2)}) async-start(), calls=%async_computation.2 | async-start | bytes 3342336 | tf_op jit(solution)/shard_map/reduce_scatter | solution.py:29
  24.2 80.4 %all-gather.15.cloned.1.call-start = ((), (), s32[]{:S(2)}) async-start(), calls=%async_computation.4 | async-start | bytes 3145728 | tf_op jit(solution)/shard_map/all_gather | solution.py:36
  26.6 127.5 %all-gather.13.cloned.1.call-start = ((), (), s32[]{:S(2)}) async-start(), calls=%async_computation.3 | async-start | bytes 3342336 | tf_op jit(solution)/shard_map/all_gather | solution.py:30
  104.5 98.3 %all-gather.23.cloned.1.call-start = ((), (), s32[]{:S(2)}) async-start(), calls=%async_computation.9 | async-start | bytes 5242880 | tf_op jit(solution)/shard_map/all_gather | solution.py:36
  107.5 139.1 %all-gather.21.cloned.1.call-start = ((), (), s32[]{:S(2)}) async-start(), calls=%async_computation.8 | async-start | bytes 2359296 | tf_op jit(solution)/shard_map/all_gather | solution.py:14
  160.0 177.5 %reduce-scatter.5.cloned.1.call-start = ((), (), s32[]{:S(2)}) async-start(), calls=%async_computation.5 | async-start | bytes 3342336 | tf_op jit(solution)/shard_map/reduce_scatter | solution.py:29
  251.1 142.2 %copy-start = (f32[12,256,256]{2,1,0:T(8,128)}, f32[12,256,256]{2,1,0:T(8,128)S(1)}, u32[]{:S(2)}) copy-start(f32[12,256,256]{2,1,0:T(8,128)S(1)} %fusion.16) | copy-start | bytes 9437188
  258.4 79.3 %all-gather.19.cloned.1.call-start = ((), (), s32[]{:S(2)}) async-start(), calls=%async_computation.7 | async-start | bytes 3145728 | tf_op jit(solution)/shard_map/all_gather | solution.py:36
  262.7 124.4 %all-gather.17.cloned.1.call-start = ((), (), s32[]{:S(2)}) async-start(), calls=%async_computation.6 | async-start | bytes 3342336 | tf_op jit(solution)/shard_map/all_gather | solution.py:30
  337.5 98.3 %all-gather.27.cloned.1.call-start = ((), (), s32[]{:S(2)}) async-start(), calls=%async_computation.11 | async-start | bytes 5242880 | tf_op jit(solution)/shard_map/all_gather | solution.py:36
  340.6 138.8 %all-gather.25.cloned.1.call-start = ((), (), s32[]{:S(2)}) async-start(), calls=%async_computation.10 | async-start | bytes 2359296 | tf_op jit(solution)/shard_map/all_gather | solution.py:14
  393.0 1.9 copy-start.1
  393.3 3.5 slice-start
  393.3 3.5 copy-start.2
  408.9 70.5 %copy-start.3 = (f32[3072,256]{1,0:T(8,128)S(1)}, f32[3072,256]{1,0:T(8,128)}, u32[]{:S(2)}) copy-start(f32[3072,256]{1,0:T(8,128)} %all-gather.17.cloned.1.call-done) | copy-start | bytes 9437188
  479.4 3.7 copy-start.4
  479.4 3.7 copy-start.5
  479.4 3.8 copy-start.6
Sparse Core Ops, SparseCore 0:
  24.3 80.1 reduce-scatter.2
  258.5 78.8 reduce-scatter.4
Sparse Core Ops, SparseCore 1:
  26.6 38.2 all-gather.14
  104.6 49.4 all-gather.12
  155.6 47.1 all-gather.22
  204.5 42.1 all-gather.20
  262.8 35.1 all-gather.18
  337.6 49.4 all-gather.16
  388.6 47.1 all-gather.26
  437.3 42.1 all-gather.24
